TPU v7x, 32 devices: a whole 2x2x4 slice. The times are simulated.
32 devices in a mesh: dom: 8 (over z, y), feat: 4 (over x, core).
Axes of the slice: x: 2, y: 2, z: 4, core: 2. Of those that a mesh axis runs over, the one named last changes fastest.
Arguments:
- nodes: bfloat16 [8192, 512], P('dom'), may hold values from -36 to 36
- walk_state: bfloat16 [8192, 256], P('dom', 'feat'), may hold values from -6 to 6
- walk_values: bfloat16 [64, 8, 128, 128], P('dom'), may hold values from -0.1875 to 0.1875
- walk_cols: int32 [64, 8], P('dom'), may hold values from 0 to 63, as said below
- walk_count: int32 [64], P('dom'), may hold values from 1 to 8
- attn_cols: int32 [64, 8], P('dom'), may hold values from 0 to 63, as said below
- attn_count: int32 [64], P('dom'), may hold values from 1 to 8
- w_query: bfloat16 [512, 512], P(None, 'feat'), may hold values from -0.25 to 0.25
- w_key: bfloat16 [512, 512], P(None, 'feat'), may hold values from -0.25 to 0.25
- w_value: bfloat16 [512, 512], P(None, 'feat'), may hold values from -0.25 to 0.25
- bias_query: bfloat16 [2, 256, 512], P(None, 'feat'), may hold values from -0.25 to 0.25
- bias_key: bfloat16 [2, 256, 512], P(None, 'feat'), may hold values from -0.25 to 0.25
- w_out: bfloat16 [512, 512], P('feat'), may hold values from -0.75 to 0.75
Outputs:
- new_nodes: bfloat16 [8192, 512], P('dom', 'feat')
- walk_next: bfloat16 [8192, 256], P('dom', 'feat')
Inputs may be any that keep to these rules, and one draw needn't show every extreme that they name: `walk_cols`: A column block of row block b lies in partitions b // 8 - 2 to b // 8 + 2, taken cyclically over the 8 partitions; slot 0 is b itself. `attn_cols`: A key block of row block b lies in partitions b // 8 - 2 to b // 8 + 2, taken cyclically over the 8 partitions; slot 0 is b itself.
All inputs are finite; a program needn't handle non-finite values.
Results may differ from a plain program's by a relative error of at most 0.015.
The roundings to bfloat16 on the way count: a program that leaves them out, or rounds other values in their place, can miss the bound.
Values may be sent and summed in bfloat16 or wider, within the bound.
A program may use at most 64 MiB of HBM per device.

v0:
```python
import math

import jax
import jax.numpy as jnp
from jax import lax
from jax.sharding import PartitionSpec as P

HD = 64
BR = 64
BS = 128
EMAX = 8
EA = 8
R = 2


def from_behind(value, axis, steps):
    count = lax.axis_size(axis)
    pairs = [(source, (source + steps) % count) for source in range(count)]
    return lax.ppermute(value, axis, pairs)


def window(shard, mover):
    pieces = []
    for offset in range(R, -R - 1, -1):
        if offset == 0:
            pieces.append(shard)
        else:
            pieces.append(mover(shard, offset))
    return jnp.concatenate(pieces, axis=0)


def propagate(wide_state, walk_values, walk_cols, walk_count, local_index):
    state_blocks = wide_state.reshape(-1, BS, wide_state.shape[1])
    near_blocks = state_blocks[local_index(walk_cols)]
    live_slot = jnp.arange(EMAX)[None, :] < walk_count[:, None]
    block_vals = jnp.where(live_slot[:, :, None, None], walk_values, jnp.zeros_like(walk_values))
    result = jnp.einsum(
        "beij,bejk->bik", block_vals, near_blocks, preferred_element_type=jnp.float32
    )
    return result.reshape(-1, wide_state.shape[1]).astype(jnp.bfloat16)


def on_device(
    nodes,
    walk_state,
    walk_values,
    walk_cols,
    walk_count,
    attn_cols,
    attn_count,
    w_query,
    w_key,
    w_value,
    bias_query,
    bias_key,
    w_out,
):
    local_blocks = walk_values.shape[0]
    local_rows = local_blocks * BS
    total_blocks = lax.axis_size("dom") * local_blocks
    first_block = (lax.axis_index("dom") - R) * local_blocks

    def local_index(block_ids):
        return jnp.mod(block_ids - first_block, total_blocks)

    wide_state = window(walk_state, lambda shard, offset: from_behind(shard, "dom", offset))
    walk_one = propagate(wide_state, walk_values, walk_cols, walk_count, local_index)
    wide_one = window(walk_one, lambda shard, offset: from_behind(shard, "dom", offset))
    walk_next = propagate(wide_one, walk_values, walk_cols, walk_count, local_index)
    feats = jnp.stack([walk_one, walk_next], axis=1)
    term_query = jnp.einsum("nsk,skc->nc", feats, bias_query, preferred_element_type=jnp.float32)
    term_key = jnp.einsum("nsk,skc->nc", feats, bias_key, preferred_element_type=jnp.float32)
    summed_query, summed_key = (
        lax.psum_scatter(
            term_query.astype(jnp.bfloat16), "feat", scatter_dimension=1, tiled=True
        ).astype(jnp.float32),
        lax.psum_scatter(
            term_key.astype(jnp.bfloat16), "feat", scatter_dimension=1, tiled=True
        ).astype(jnp.float32),
    )
    bias_q = summed_query.astype(jnp.bfloat16)
    bias_k = summed_key.astype(jnp.bfloat16)
    queries = jnp.dot(nodes, w_query, preferred_element_type=jnp.float32).astype(jnp.bfloat16)
    head_width = w_query.shape[1]
    keys = jnp.dot(nodes, w_key, preferred_element_type=jnp.float32).astype(jnp.bfloat16)
    vals = jnp.dot(nodes, w_value, preferred_element_type=jnp.float32).astype(jnp.bfloat16)
    packed = jnp.concatenate([keys, vals, bias_k], axis=1)
    wide_pack = window(packed, lambda shard, offset: from_behind(shard, "dom", offset))
    key_window = wide_pack[:, :head_width]
    value_window = wide_pack[:, head_width : 2 * head_width]
    bias_window = wide_pack[:, 2 * head_width :]
    head_count = head_width // HD
    window_blocks = key_window.shape[0] // BS
    key_blocks = key_window.reshape(window_blocks, BS, head_count, HD)
    value_blocks = value_window.reshape(window_blocks, BS, head_count, HD)
    bias_blocks = bias_window.reshape(window_blocks, BS, head_count, BR)
    group_size = math.gcd(local_blocks, 4)
    group_total = local_blocks // group_size
    query_groups = queries.reshape(group_total, group_size, BS, head_count, HD)
    bias_groups = bias_q.reshape(group_total, group_size, BS, head_count, BR)
    block_groups = attn_cols.reshape(group_total, group_size, EA)
    count_groups = attn_count.reshape(group_total, group_size)

    def attend(inputs):
        query_rows, bias_rows, block_ids, slot_count = inputs
        position = local_index(block_ids)
        key_near = key_blocks[position]
        value_near = value_blocks[position]
        bias_near = bias_blocks[position]
        scores = jnp.einsum(
            "gihd,gejhd->ghiej", query_rows, key_near, preferred_element_type=jnp.float32
        ) * HD ** (-0.5)
        scores = scores + jnp.einsum(
            "gihr,gejhr->ghiej", bias_rows, bias_near, preferred_element_type=jnp.float32
        ) * BR ** (-0.5)
        live_slot = (jnp.arange(EA)[None, :] < slot_count[:, None])[:, None, None, :, None]
        scores = jnp.where(live_slot, scores, -1e30)
        top_score = jnp.max(scores, axis=(3, 4), keepdims=True)
        expo = jnp.exp(scores - top_score)
        weights = (expo / jnp.sum(expo, axis=(3, 4), keepdims=True)).astype(jnp.bfloat16)
        return jnp.einsum(
            "ghiej,gejhd->gihd", weights, value_near, preferred_element_type=jnp.float32
        ).astype(jnp.bfloat16)

    attended = lax.map(attend, (query_groups, bias_groups, block_groups, count_groups)).reshape(
        local_rows, head_width
    )
    out_term = jnp.dot(attended, w_out, preferred_element_type=jnp.float32)
    new_nodes = lax.psum_scatter(
        out_term.astype(jnp.bfloat16), "feat", scatter_dimension=1, tiled=True
    )
    return (new_nodes, walk_next)


def solution(mesh):
    placed = (
        P("dom", None),
        P("dom", "feat"),
        P("dom", None, None, None),
        P("dom", None),
        P("dom"),
        P("dom", None),
        P("dom"),
        P(None, "feat"),
        P(None, "feat"),
        P(None, "feat"),
        P(None, "feat", None),
        P(None, "feat", None),
        P("feat", None),
    )
    return jax.shard_map(
        on_device,
        mesh=mesh,
        in_specs=placed,
        out_specs=(P("dom", "feat"), P("dom", "feat")),
        check_vma=False,
    )
```

profile of v0, /device:TPU:0, one launch (start us, length us, event | category | flops | bytes accessed | tf_op | source)
XLA Modules:
  0.0 245.3 jit_solution(13656822220974705130)
XLA Ops:
  7.2 3.1 %collective-permute-start = (bf16[1024,64]{0,1:T(8,128)(2,1)}, bf16[1024,64]{0,1:T(8,128)(2,1)S(1)}, u32[]{:S(2)}, u32[]{:S(2)}) collective-permute-start(bf16[1024,64]{0,1:T(8,128)(2,1)} %param.16), channel_id=1, source_target_pairs={{0,8},{4,12},{8,16},{12,20},{16,24},{20,28},{24,0},{28,4},{1,9},{5... | collective-permute-start | bytes 393224 | tf_op jit(solution)/shard_map/ppermute | solution.py:19
  10.3 1.5 collective-permute-start.1
  11.8 3.2 %collective-permute-start.2 = (bf16[1024,64]{0,1:T(8,128)(2,1)}, bf16[1024,64]{0,1:T(8,128)(2,1)S(1)}, u32[]{:S(2)}, u32[]{:S(2)}) collective-permute-start(bf16[1024,64]{0,1:T(8,128)(2,1)} %param.16), channel_id=1, source_target_pairs={{0,28},{4,0},{8,4},{12,8},{16,12},{20,16},{24,20},{28,24},{1,29},{... | collective-permute-start | bytes 393224 | tf_op jit(solution)/shard_map/ppermute | solution.py:19
  16.9 4.1 %collective-permute-done.1 = bf16[1024,64]{0,1:T(8,128)(2,1)S(1)} collective-permute-done((bf16[1024,64]{0,1:T(8,128)(2,1)}, bf16[1024,64]{0,1:T(8,128)(2,1)S(1)}, u32[]{:S(2)}, u32[]{:S(2)}) %collective-permute-start.1) | collective-permute-done | bytes 131104 | tf_op jit(solution)/shard_map/ppermute | solution.py:19
  22.8 2.5 %fusion.25 = bf16[8,128,64]{1,2,0:T(8,128)(2,1)S(1)} fusion(bf16[8,8,128,64]{2,3,1,0:T(8,128)(2,1)S(1)} %bitcast.148, bf16[8,8,128,128]{3,2,1,0:T(8,128)(2,1)} %param.17, pred[8,8]{1,0:T(8,128)(4,1)S(1)} %iota_compare_fusion.1), kind=kOutput, calls=%fused_computation.47 | convolution fusion | flops 135331840 | bytes 3276864 | tf_op jit(solution)/shard_map/beij,bejk->bik/dot_general | solution.py:37
  25.9 1.4 collective-permute-start.5
  27.3 3.3 %collective-permute-start.6 = (bf16[1024,64]{0,1:T(8,128)(2,1)S(1)}, bf16[1024,64]{0,1:T(8,128)(2,1)S(1)}, u32[]{:S(2)}, u32[]{:S(2)}) collective-permute-start(bf16[1024,64]{0,1:T(8,128)(2,1)S(1)} %copy_bitcast_fusion.5), channel_id=1, source_target_pairs={{0,28},{4,0},{8,4},{12,8},{16,12},{20,16},{24,20},{28,24},{1,29},{... | collective-permute-start | bytes 393224 | tf_op jit(solution)/shard_map/ppermute | solution.py:19
  30.6 1.6 collective-permute-start.7
  33.0 4.2 %collective-permute-done.5 = bf16[1024,64]{0,1:T(8,128)(2,1)S(1)} collective-permute-done((bf16[1024,64]{0,1:T(8,128)(2,1)S(1)}, bf16[1024,64]{0,1:T(8,128)(2,1)S(1)}, u32[]{:S(2)}, u32[]{:S(2)}) %collective-permute-start.5) | collective-permute-done | bytes 131104 | tf_op jit(solution)/shard_map/ppermute | solution.py:19
  38.4 2.5 %fusion.24 = bf16[8,128,64]{1,2,0:T(8,128)(2,1)S(1)} fusion(bf16[8,8,128,64]{2,3,1,0:T(8,128)(2,1)S(1)} %bitcast.147, bf16[8,8,128,128]{3,2,1,0:T(8,128)(2,1)} %param.17, pred[8,8]{1,0:T(8,128)(4,1)S(1)} %iota_compare_fusion.1), kind=kOutput, calls=%fused_computation.46 | convolution fusion | flops 135331840 | bytes 3276864 | tf_op jit(solution)/shard_map/beij,bejk->bik/dot_general | solution.py:37
  41.2 1.5 bitcast_convert_fusion.1
  43.2 1.3 copy.93
  45.6 21.1 %reduce-scatter.8.cloned.1.call-done = bf16[1024,128]{0,1:T(8,128)(2,1)} async-done(((bf16[1024,512]{0,1:T(8,128)(2,1)}), bf16[1024,128]{0,1:T(8,128)(2,1)}) %reduce-scatter.8.cloned.1.call-update) | async-done | bytes 262160 | tf_op jit(solution)/shard_map/reduce_scatter | solution.py:77
  67.7 1.5 collective-permute-start.8
  69.2 1.5 collective-permute-start.9
  70.7 3.3 %collective-permute-start.10 = (bf16[1024,384]{0,1:T(8,128)(2,1)S(1)}, bf16[1024,384]{0,1:T(8,128)(2,1)}, u32[]{:S(2)}, u32[]{:S(2)}) collective-permute-start(bf16[1024,384]{0,1:T(8,128)(2,1)S(1)} %pad_maximum_fusion), channel_id=1, source_target_pairs={{0,28},{4,0},{8,4},{12,8},{16,12},{20,16},{24,20},{28,24},{1,29},{... | collective-permute-start | bytes 2359304 | tf_op jit(solution)/shard_map/ppermute | solution.py:19
  76.2 18.1 %reduce-scatter.10.cloned.1.call-done = bf16[128,1024]{1,0:T(8,128)(2,1)} async-done(((bf16[512,1024]{1,0:T(8,128)(2,1)}), bf16[128,1024]{1,0:T(8,128)(2,1)}) %reduce-scatter.10.cloned.1.call-update) | async-done | bytes 262160
  94.3 1.8 reshape.232
  96.1 1.2 constant_dynamic-update-slice_fusion.16
  97.3 10.6 %collective-permute-done.9 = bf16[1024,384]{0,1:T(8,128)(2,1)} collective-permute-done((bf16[1024,384]{0,1:T(8,128)(2,1)S(1)}, bf16[1024,384]{0,1:T(8,128)(2,1)}, u32[]{:S(2)}, u32[]{:S(2)}) %collective-permute-start.9) | collective-permute-done | bytes 786464 | tf_op jit(solution)/shard_map/ppermute | solution.py:19
  107.9 1.2 constant_dynamic-update-slice_fusion.15
  109.1 1.2 constant_dynamic-update-slice_fusion.13
  110.3 12.3 %collective-permute-done.11 = bf16[1024,384]{0,1:T(8,128)(2,1)} collective-permute-done((bf16[1024,384]{0,1:T(8,128)(2,1)S(1)}, bf16[1024,384]{0,1:T(8,128)(2,1)}, u32[]{:S(2)}, u32[]{:S(2)}) %collective-permute-start.11) | collective-permute-done | bytes 786464 | tf_op jit(solution)/shard_map/ppermute | solution.py:19
  123.8 1.8 slice_bitcast_fusion
  125.8 3.5 %copy.74 = bf16[40,128,2,64]{3,2,1,0:T(2,128)(2,1)} copy(bf16[40,128,2,64]{1,0,3,2:T(8,128)(2,1)S(1)} %bitcast.144) | data formatting | bytes 2621440 | tf_op jit(solution)/shard_map/while | solution.py:125
  129.3 1.6 copy.107
  130.9 3.5 %copy.76 = bf16[40,128,2,64]{3,2,1,0:T(2,128)(2,1)} copy(bf16[40,128,2,64]{1,0,3,2:T(8,128)(2,1)S(1)} %bitcast.145) | data formatting | bytes 2621440 | tf_op jit(solution)/shard_map/while | solution.py:125
  134.4 1.6 copy.108
  136.0 3.5 %copy.78 = bf16[40,128,2,64]{3,2,1,0:T(2,128)(2,1)} copy(bf16[40,128,2,64]{1,0,3,2:T(8,128)(2,1)S(1)} %bitcast.146) | data formatting | bytes 2621440 | tf_op jit(solution)/shard_map/while | solution.py:125
  139.5 70.3 %while.12 = (s32[]{:T(128)}, bf16[2,4,128,2,64]{2,1,0,4,3:T(4,128)(2,1)}, s32[2,4,8]{2,1,0:T(4,128)S(1)}, s32[]{:T(128)}, bf16[40,128,2,64]{3,2,1,0:T(2,128)(2,1...) while((s32[]{:T(128)}, ...), condition=%wide.region_5.6_spmd, body=%wide.region_2.5_spmd.sunk | while | flops 412155392 | bytes 49178380 | solution.py:125
  139.6 7.2 %gather_fusion = bf16[32,128,2,64]{3,2,1,0:T(2,128)(2,1)S(1)} fusion(bf16[40,128,2,64]{3,2,1,0:T(2,128)(2,1)} %get-tuple-element.288, s32[1024]{0:T(1024)S(1)} %pad_clamp_fusion.3), kind=kCustom, calls=%fused_computation.1.clone.1 | custom fusion | bytes 2097280 | tf_op jit(solution)/shard_map/while/body/eval_jaxpr/gather | solution.py:107
  146.8 2.6 %fusion.62 = f32[4,2,128,8,128]{2,4,3,1,0:T(8,128)} fusion(bf16[4,8,128,2,64]{4,3,2,1,0:T(2,128)(2,1)S(1)} %bitcast.142, bf16[2,4,128,2,64]{2,4,3,1,0:T(8,128)(2,1)S(1)} %get-tuple-element.287, s32[]{:T(128)} %get-tuple-element.270), kind=kOutput, calls=%fused_computation.12.clone.1 | convolution fusion | flops 134217728 | bytes 6422532 | tf_op jit(solution)/shard_map/while/body/eval_jaxpr/gihd,gejhd->ghiej/dot_general | solution.py:110
  149.4 7.2 %gather_fusion.1 = bf16[32,128,2,64]{3,2,1,0:T(2,128)(2,1)S(1)} fusion(bf16[40,128,2,64]{3,2,1,0:T(2,128)(2,1)} %get-tuple-element.290, s32[1024]{0:T(1024)S(1)} %pad_clamp_fusion.3), kind=kCustom, calls=%fused_computation.2.clone.1 | custom fusion | bytes 2097280 | tf_op jit(solution)/shard_map/while/body/eval_jaxpr/gather | solution.py:109
  158.3 3.0 %fusion.64 = (f32[4,2,128]{2,1,0:T(2,128)S(1)}, f32[4,2,128,8,128]{2,4,3,1,0:T(8,128)S(1)}) fusion(f32[4,2,128,8,128]{2,4,3,1,0:T(8,128)} %fusion.62, bf16[4,8,128,2,64]{4,3,2,1,0:T(2,128)(2,1)S(1)} %bitcast.141, bf16[1,4,128,2,64]{2,1,0,4,3:T(4,128)(2,1)S(1)} %constant_dynamic-slice_fusion.3, pred[4,8]{1,0:T(4,128)(4,1)S(1)} %iota_compare_fusion.3), kind=kOutput, calls=%fused_computation.81.clone.1 | convolution fusion | flops 138411008 | bytes 9572384 | tf_op jit(solution)/shard_map/while/body/eval_jaxpr/gihr,gejhr->ghiej/dot_general | solution.py:113
  161.9 1.4 copy-done.1
  163.3 7.2 %gather_fusion.2 = bf16[32,128,2,64]{3,2,1,0:T(2,128)(2,1)S(1)} fusion(bf16[40,128,2,64]{3,2,1,0:T(2,128)(2,1)} %get-tuple-element.285, s32[1024]{0:T(1024)S(1)} %pad_clamp_fusion.3), kind=kCustom, calls=%fused_computation.clone.1 | custom fusion | bytes 2097280 | tf_op jit(solution)/shard_map/while/body/eval_jaxpr/gather | solution.py:108
  170.5 3.4 %fusion.66 = bf16[1,4,128,2,64]{2,4,3,1,0:T(8,128)(2,1)S(1)} fusion(f32[4,2,128,8,128]{2,4,3,1,0:T(8,128)} %copy-done.1, f32[4,2,128]{2,1,0:T(2,128)S(1)} %fusion.65, f32[4,2,128]{2,1,0:T(2,128)S(1)} %get-tuple-element.258, bf16[4,8,128,2,64]{4,3,2,1,0:T(2,128)(2,1)S(1)} %bitcast.143), kind=kOutput, calls=%fused_computation.16.clone.1 | convolution fusion | flops 137428992 | bytes 5382144 | tf_op jit(solution)/shard_map/while/body/eval_jaxpr/ghiej,gejhd->gihd/dot_general | solution.py:121
  174.8 7.2 %gather_fusion = bf16[32,128,2,64]{3,2,1,0:T(2,128)(2,1)S(1)} fusion(bf16[40,128,2,64]{3,2,1,0:T(2,128)(2,1)} %get-tuple-element.288, s32[1024]{0:T(1024)S(1)} %pad_clamp_fusion.3), kind=kCustom, calls=%fused_computation.1.clone.1 | custom fusion | bytes 2097280 | tf_op jit(solution)/shard_map/while/body/eval_jaxpr/gather | solution.py:107
  182.0 2.6 %fusion.62 = f32[4,2,128,8,128]{2,4,3,1,0:T(8,128)} fusion(bf16[4,8,128,2,64]{4,3,2,1,0:T(2,128)(2,1)S(1)} %bitcast.142, bf16[2,4,128,2,64]{2,4,3,1,0:T(8,128)(2,1)S(1)} %get-tuple-element.287, s32[]{:T(128)} %get-tuple-element.270), kind=kOutput, calls=%fused_computation.12.clone.1 | convolution fusion | flops 134217728 | bytes 6422532 | tf_op jit(solution)/shard_map/while/body/eval_jaxpr/gihd,gejhd->ghiej/dot_general | solution.py:110
  184.6 7.2 %gather_fusion.1 = bf16[32,128,2,64]{3,2,1,0:T(2,128)(2,1)S(1)} fusion(bf16[40,128,2,64]{3,2,1,0:T(2,128)(2,1)} %get-tuple-element.290, s32[1024]{0:T(1024)S(1)} %pad_clamp_fusion.3), kind=kCustom, calls=%fused_computation.2.clone.1 | custom fusion | bytes 2097280 | tf_op jit(solution)/shard_map/while/body/eval_jaxpr/gather | solution.py:109
  193.5 3.0 %fusion.64 = (f32[4,2,128]{2,1,0:T(2,128)S(1)}, f32[4,2,128,8,128]{2,4,3,1,0:T(8,128)S(1)}) fusion(f32[4,2,128,8,128]{2,4,3,1,0:T(8,128)} %fusion.62, bf16[4,8,128,2,64]{4,3,2,1,0:T(2,128)(2,1)S(1)} %bitcast.141, bf16[1,4,128,2,64]{2,1,0,4,3:T(4,128)(2,1)S(1)} %constant_dynamic-slice_fusion.3, pred[4,8]{1,0:T(4,128)(4,1)S(1)} %iota_compare_fusion.3), kind=kOutput, calls=%fused_computation.81.clone.1 | convolution fusion | flops 138411008 | bytes 9572384 | tf_op jit(solution)/shard_map/while/body/eval_jaxpr/gihr,gejhr->ghiej/dot_general | solution.py:113
  197.1 1.4 copy-done.1
  198.5 7.2 %gather_fusion.2 = bf16[32,128,2,64]{3,2,1,0:T(2,128)(2,1)S(1)} fusion(bf16[40,128,2,64]{3,2,1,0:T(2,128)(2,1)} %get-tuple-element.285, s32[1024]{0:T(1024)S(1)} %pad_clamp_fusion.3), kind=kCustom, calls=%fused_computation.clone.1 | custom fusion | bytes 2097280 | tf_op jit(solution)/shard_map/while/body/eval_jaxpr/gather | solution.py:108
  205.7 3.4 %fusion.66 = bf16[1,4,128,2,64]{2,4,3,1,0:T(8,128)(2,1)S(1)} fusion(f32[4,2,128,8,128]{2,4,3,1,0:T(8,128)} %copy-done.1, f32[4,2,128]{2,1,0:T(2,128)S(1)} %fusion.65, f32[4,2,128]{2,1,0:T(2,128)S(1)} %get-tuple-element.258, bf16[4,8,128,2,64]{4,3,2,1,0:T(2,128)(2,1)S(1)} %bitcast.143), kind=kOutput, calls=%fused_computation.16.clone.1 | convolution fusion | flops 137428992 | bytes 5382144 | tf_op jit(solution)/shard_map/while/body/eval_jaxpr/ghiej,gejhd->gihd/dot_general | solution.py:121
  210.9 1.4 convolution_convert_fusion
  212.3 1.3 copy.95
  214.3 22.6 %reduce-scatter.12.cloned.1.call-done = bf16[128,1024]{1,0:T(8,128)(2,1)} async-done(((bf16[512,1024]{1,0:T(8,128)(2,1)}), bf16[128,1024]{1,0:T(8,128)(2,1)}) %reduce-scatter.12.cloned.1.call-update) | async-done | bytes 262160
  237.0 1.8 copy.96
  (92 shorter events, 20.9 us)
Async XLA Ops:
  7.2 37.5 %copy-start = (bf16[1024,512]{1,0:T(8,128)(2,1)S(1)}, bf16[1024,512]{1,0:T(8,128)(2,1)}, u32[]{:S(2)}) copy-start(bf16[1024,512]{1,0:T(8,128)(2,1)} %param.15) | copy-start | bytes 3145732
  7.2 59.5 %reduce-scatter.8.cloned.1.call-start = ((), (), s32[]{:S(2)}) async-start(), calls=%async_computation.3 | async-start | bytes 1310720 | tf_op jit(solution)/shard_map/reduce_scatter | solution.py:77
  7.2 9.6 %collective-permute-start = (bf16[1024,64]{0,1:T(8,128)(2,1)}, bf16[1024,64]{0,1:T(8,128)(2,1)S(1)}, u32[]{:S(2)}, u32[]{:S(2)}) collective-permute-start(bf16[1024,64]{0,1:T(8,128)(2,1)} %param.16), channel_id=1, source_target_pairs={{0,8},{4,12},{8,16},{12,20},{16,24},{20,28},{24,0},{28,4},{1,9},{5... | collective-permute-start | bytes 393224 | tf_op jit(solution)/shard_map/ppermute | solution.py:19
  10.3 10.6 %collective-permute-start.1 = (bf16[1024,64]{0,1:T(8,128)(2,1)}, bf16[1024,64]{0,1:T(8,128)(2,1)S(1)}, u32[]{:S(2)}, u32[]{:S(2)}) collective-permute-start(bf16[1024,64]{0,1:T(8,128)(2,1)} %param.16), channel_id=1, source_target_pairs={{0,4},{4,8},{8,12},{12,16},{16,20},{20,24},{24,28},{28,0},{1,5},{5... | collective-permute-start | bytes 393224 | tf_op jit(solution)/shard_map/ppermute | solution.py:19
  11.8 10.0 %collective-permute-start.2 = (bf16[1024,64]{0,1:T(8,128)(2,1)}, bf16[1024,64]{0,1:T(8,128)(2,1)S(1)}, u32[]{:S(2)}, u32[]{:S(2)}) collective-permute-start(bf16[1024,64]{0,1:T(8,128)(2,1)} %param.16), channel_id=1, source_target_pairs={{0,28},{4,0},{8,4},{12,8},{16,12},{20,16},{24,20},{28,24},{1,29},{... | collective-permute-start | bytes 393224 | tf_op jit(solution)/shard_map/ppermute | solution.py:19
  15.0 6.9 %collective-permute-start.3 = (bf16[1024,64]{0,1:T(8,128)(2,1)}, bf16[1024,64]{0,1:T(8,128)(2,1)S(1)}, u32[]{:S(2)}, u32[]{:S(2)}) collective-permute-start(bf16[1024,64]{0,1:T(8,128)(2,1)} %param.16), channel_id=1, source_target_pairs={{0,24},{4,28},{8,0},{12,4},{16,8},{20,12},{24,16},{28,20},{1,25},{... | collective-permute-start | bytes 393224 | tf_op jit(solution)/shard_map/ppermute | solution.py:19
  25.4 7.6 %collective-permute-start.4 = (bf16[1024,64]{0,1:T(8,128)(2,1)S(1)}, bf16[1024,64]{0,1:T(8,128)(2,1)S(1)}, u32[]{:S(2)}, u32[]{:S(2)}) collective-permute-start(bf16[1024,64]{0,1:T(8,128)(2,1)S(1)} %copy_bitcast_fusion.5), channel_id=1, source_target_pairs={{0,8},{4,12},{8,16},{12,20},{16,24},{20,28},{24,0},{28,4},{1,9},{5... | collective-permute-start | bytes 393224 | tf_op jit(solution)/shard_map/ppermute | solution.py:19
  25.9 11.3 %collective-permute-start.5 = (bf16[1024,64]{0,1:T(8,128)(2,1)S(1)}, bf16[1024,64]{0,1:T(8,128)(2,1)S(1)}, u32[]{:S(2)}, u32[]{:S(2)}) collective-permute-start(bf16[1024,64]{0,1:T(8,128)(2,1)S(1)} %copy_bitcast_fusion.5), channel_id=1, source_target_pairs={{0,4},{4,8},{8,12},{12,16},{16,20},{20,24},{24,28},{28,0},{1,5},{5... | collective-permute-start | bytes 393224 | tf_op jit(solution)/shard_map/ppermute | solution.py:19
  27.3 9.9 %collective-permute-start.6 = (bf16[1024,64]{0,1:T(8,128)(2,1)S(1)}, bf16[1024,64]{0,1:T(8,128)(2,1)S(1)}, u32[]{:S(2)}, u32[]{:S(2)}) collective-permute-start(bf16[1024,64]{0,1:T(8,128)(2,1)S(1)} %copy_bitcast_fusion.5), channel_id=1, source_target_pairs={{0,28},{4,0},{8,4},{12,8},{16,12},{20,16},{24,20},{28,24},{1,29},{... | collective-permute-start | bytes 393224 | tf_op jit(solution)/shard_map/ppermute | solution.py:19
  30.6 6.9 %collective-permute-start.7 = (bf16[1024,64]{0,1:T(8,128)(2,1)S(1)}, bf16[1024,64]{0,1:T(8,128)(2,1)S(1)}, u32[]{:S(2)}, u32[]{:S(2)}) collective-permute-start(bf16[1024,64]{0,1:T(8,128)(2,1)S(1)} %copy_bitcast_fusion.5), channel_id=1, source_target_pairs={{0,24},{4,28},{8,0},{12,4},{16,8},{20,12},{24,16},{28,20},{1,25},{... | collective-permute-start | bytes 393224 | tf_op jit(solution)/shard_map/ppermute | solution.py:19
  38.4 2.8 %copy-start.3 = (bf16[2,64,512]{2,1,0:T(8,128)(2,1)S(1)}, bf16[2,64,512]{2,1,0:T(8,128)(2,1)}, u32[]{:S(2)}) copy-start(bf16[2,64,512]{2,1,0:T(8,128)(2,1)} %param.26) | copy-start | bytes 393220
  41.0 1.8 copy-start.4
  42.7 2.0 copy-start.5
  42.7 51.6 %reduce-scatter.10.cloned.1.call-start = ((), (), s32[]{:S(2)}) async-start(), calls=%async_computation.4 | async-start | bytes 1310720
  43.2 1.9 copy-start.6
  44.6 29.9 %copy-start.7 = (bf16[512,128]{1,0:T(8,128)(2,1)S(1)}, bf16[512,128]{1,0:T(8,128)(2,1)}, u32[]{:S(2)}) copy-start(bf16[512,128]{1,0:T(8,128)(2,1)} %param.22) | copy-start | bytes 393220
  44.6 192.4 %reduce-scatter.12.cloned.1.call-start = ((), (), s32[]{:S(2)}) async-start(), calls=%async_computation.5 | async-start | bytes 1310720
  45.6 29.9 %copy-start.9 = (s32[8]{0:T(128)S(1)}, s32[8]{0:T(128)}, u32[]{:S(2)}) copy-start(s32[8]{0:T(128)} %param.21) | copy-start | bytes 100
  67.7 28.4 %collective-permute-start.8 = (bf16[1024,384]{0,1:T(8,128)(2,1)S(1)}, bf16[1024,384]{0,1:T(8,128)(2,1)}, u32[]{:S(2)}, u32[]{:S(2)}) collective-permute-start(bf16[1024,384]{0,1:T(8,128)(2,1)S(1)} %pad_maximum_fusion), channel_id=1, source_target_pairs={{0,8},{4,12},{8,16},{12,20},{16,24},{20,28},{24,0},{28,4},{1,9},{5... | collective-permute-start | bytes 2359304 | tf_op jit(solution)/shard_map/ppermute | solution.py:19
  69.2 38.7 %collective-permute-start.9 = (bf16[1024,384]{0,1:T(8,128)(2,1)S(1)}, bf16[1024,384]{0,1:T(8,128)(2,1)}, u32[]{:S(2)}, u32[]{:S(2)}) collective-permute-start(bf16[1024,384]{0,1:T(8,128)(2,1)S(1)} %pad_maximum_fusion), channel_id=1, source_target_pairs={{0,4},{4,8},{8,12},{12,16},{16,20},{20,24},{24,28},{28,0},{1,5},{5... | collective-permute-start | bytes 2359304 | tf_op jit(solution)/shard_map/ppermute | solution.py:19
  70.7 38.4 %collective-permute-start.10 = (bf16[1024,384]{0,1:T(8,128)(2,1)S(1)}, bf16[1024,384]{0,1:T(8,128)(2,1)}, u32[]{:S(2)}, u32[]{:S(2)}) collective-permute-start(bf16[1024,384]{0,1:T(8,128)(2,1)S(1)} %pad_maximum_fusion), channel_id=1, source_target_pairs={{0,28},{4,0},{8,4},{12,8},{16,12},{20,16},{24,20},{28,24},{1,29},{... | collective-permute-start | bytes 2359304 | tf_op jit(solution)/shard_map/ppermute | solution.py:19
  73.9 48.7 %collective-permute-start.11 = (bf16[1024,384]{0,1:T(8,128)(2,1)S(1)}, bf16[1024,384]{0,1:T(8,128)(2,1)}, u32[]{:S(2)}, u32[]{:S(2)}) collective-permute-start(bf16[1024,384]{0,1:T(8,128)(2,1)S(1)} %pad_maximum_fusion), channel_id=1, source_target_pairs={{0,24},{4,28},{8,0},{12,4},{16,8},{20,12},{24,16},{28,20},{1,25},{... | collective-permute-start | bytes 2359304 | tf_op jit(solution)/shard_map/ppermute | solution.py:19
  75.2 33.9 %copy-start.2 = (bf16[1024,128]{0,1:T(8,128)(2,1)S(1)}, bf16[1024,128]{0,1:T(8,128)(2,1)}, u32[]{:S(2)}) copy-start(bf16[1024,128]{0,1:T(8,128)(2,1)} %reduce-scatter.8.cloned.1.call-done) | copy-start | bytes 786436
  136.0 3.5 %copy-start.8 = (s32[8,8]{1,0:T(8,128)S(1)}, s32[8,8]{1,0:T(8,128)}, u32[]{:S(2)}) copy-start(s32[8,8]{1,0:T(8,128)} %param.20) | copy-start | bytes 772
  161.4 2.0 copy-start.1
  196.5 2.0 copy-start.1
Sparse Core Ops, SparseCore 0:
  42.8 23.8 reduce-scatter.7
  69.4 24.8 reduce-scatter.9
  213.8 23.1 reduce-scatter.11
where the time goes:
time: 246 us; the launch traced here: 245 us
  waiting for transfers between devices  93.8 us (38%)
  local copies, waits for them, and re-layouts  83.8 us (34%)
  matrix products  27.8 us (11%)
  starting transfers between devices  21.8 us (9%)
  between operations  14.2 us (6%)
  other arithmetic  3.81 us (2%)
    unnamed x5, waiting for transfers between devices  40.8 us
    ppermute x12, waiting for transfers between devices, from_behind(): return lax.ppermute(value, axis, pairs)  32 us
    ppermute x12, starting transfers between devices, from_behind(): return lax.ppermute(value, axis, pairs)  21.7 us
    reduce_scatter x1, waiting for transfers between devices, on_device(): lax.psum_scatter(term_key.astype(jnp.bfloat16), 'feat', scatter_dimension...  21.1 us
    gather x2, local copies, waits for them, and re-layouts, attend(): key_near = key_blocks[position]  14.4 us
    gather x2, local copies, waits for them, and re-layouts, attend(): bias_near = bias_blocks[position]  14.4 us
    gather x2, local copies, waits for them, and re-layouts, attend(): value_near = value_blocks[position]  14.4 us
    unnamed x37, local copies, waits for them, and re-layouts  14.2 us
  transfers between devices with their start and end apart: 15, of which 9 were waited for; matrix products, arithmetic and copies ran while one was open for 6% of the time, Pallas kernels for 0%

commit v1 on v0

v1 whole, which is shorter than its diff:
```python
import functools

import jax
import jax.numpy as jnp
from jax import lax
from jax.experimental import pallas as pl
from jax.experimental.pallas import tpu as pltpu
from jax.sharding import PartitionSpec as P

HD = 64
BS = 128
R = 2
MESH = pl.DeviceIdType.MESH
OFFSETS = tuple(o for o in range(-R, R + 1) if o != 0)
LOG2E = 1.4426950408889634


def dot(left, right):
    return jnp.dot(left, right, preferred_element_type=jnp.float32)


def dot_t(left, right):
    return lax.dot_general(
        left, right, (((1,), (1,)), ((), ())), preferred_element_type=jnp.float32
    )


def kernel(
    sizes,
    walk_cols,
    walk_count,
    attn_cols,
    attn_count,
    nodes,
    walk_state,
    walk_values,
    w_query,
    w_key,
    w_value,
    bias_query,
    bias_key,
    w_out,
    new_nodes,
    walk_next,
    win0,
    win1,
    kv,
    bk,
    f1,
    f2,
    bw,
    wbd,
    queries,
    biasq,
    stage,
    landed,
    state_send,
    state_recv,
    one_send,
    one_recv,
    kv_send,
    kv_recv,
    bk_send,
    bk_recv,
    f1_send,
    f1_recv,
    f2_send,
    f2_recv,
    bw_send,
    bw_recv,
    out_send,
    out_recv,
):
    n_dom, n_feat, blocks, walk_slots, attn_slots = sizes
    half = blocks // 2
    window_blocks = (2 * R + 1) * blocks
    total = n_dom * blocks
    me_dom = lax.axis_index("dom")
    me_feat = lax.axis_index("feat")
    first = (me_dom - R) * blocks
    near = [lax.rem(me_dom + o + n_dom, n_dom) for o in OFFSETS]
    peers = [lax.rem(me_feat + d, n_feat) for d in range(1, n_feat)]
    lane = lax.broadcasted_iota(jnp.int32, (1, BS), 1)
    lane_half = lax.div(lane, HD)

    def place(block_id):
        pos = lax.rem(block_id - first + total, total)
        return jnp.minimum(pos, window_blocks - 1)

    def to_dom(buffer, per, send, recv):
        copies = []
        for i, o in enumerate(OFFSETS):
            copies.append(
                pltpu.make_async_remote_copy(
                    src_ref=buffer.at[pl.ds(R * per, per)],
                    dst_ref=buffer.at[pl.ds((R - o) * per, per)],
                    send_sem=send.at[i],
                    recv_sem=recv.at[i],
                    device_id={"dom": near[i]},
                    device_id_type=MESH,
                )
            )
        return copies

    def to_feat(buffer, per, send, recv):
        copies = []
        mine = pl.ds(me_feat * per, per)
        for i, peer in enumerate(peers):
            copies.append(
                pltpu.make_async_remote_copy(
                    src_ref=buffer.at[mine],
                    dst_ref=buffer.at[mine],
                    send_sem=send.at[i],
                    recv_sem=recv.at[i],
                    device_id={"feat": peer},
                    device_id_type=MESH,
                )
            )
        return copies

    def start(copies):
        for copy in copies:
            copy.start()

    def wait_recv(copies):
        for copy in copies:
            copy.wait_recv()

    win0[pl.ds(R * half, half)] = jnp.concatenate(
        [walk_state[: half * BS, :], walk_state[half * BS :, :]], axis=1
    ).reshape(half, BS, BS)

    barrier = pltpu.get_barrier_semaphore()
    for device in near:
        pl.semaphore_signal(barrier, inc=1, device_id={"dom": device}, device_id_type=MESH)
    for device in peers:
        pl.semaphore_signal(barrier, inc=1, device_id={"feat": device}, device_id_type=MESH)
    pl.semaphore_wait(barrier, len(near) + len(peers))

    state_copies = to_dom(win0, half, state_send, state_recv)
    start(state_copies)
    bw_copies = []
    for t, weight in enumerate((bias_query, bias_key)):
        for i, peer in enumerate(peers):
            bw_copies.append(
                pltpu.make_async_remote_copy(
                    src_ref=weight.at[:, :, pl.ds(pl.multiple_of(peer * BS, BS), BS)],
                    dst_ref=bw.at[me_feat, t],
                    send_sem=bw_send.at[t, i],
                    recv_sem=bw_recv.at[t, i],
                    device_id={"feat": peer},
                    device_id_type=MESH,
                )
            )
    start(bw_copies)

    w_all = jnp.concatenate([w_query[...], w_key[...], w_value[...]], axis=1)

    def project(i, carry):
        rows = nodes[pl.ds(pl.multiple_of(i * 2 * BS, 2 * BS), 2 * BS), :]
        product = dot(rows, w_all).astype(jnp.bfloat16)
        queries[pl.ds(2 * i, 2)] = product[:, :BS].reshape(2, BS, BS)
        kv[pl.ds(2 * R * blocks + 2 * i, 2)] = product[:, BS : 2 * BS].reshape(2, BS, BS)
        kv[pl.ds((2 * R + 1) * blocks + 2 * i, 2)] = product[:, 2 * BS :].reshape(2, BS, BS)
        return carry

    lax.fori_loop(0, blocks // 2, project, 0)

    def walk_rows(window, b):
        count = walk_count[b]
        parts = []
        for e in range(walk_slots):
            pos = place(walk_cols[b, e])
            part = lax.div(pos, blocks)
            block = lax.rem(pos, blocks)
            side = jnp.where(e < count, lax.div(block, half), 2)
            keep = jnp.where(lane_half == side, 1.0, 0.0).astype(jnp.bfloat16)
            parts.append(window[part * half + lax.rem(block, half)] * keep)
        left = jnp.concatenate([walk_values[b, e] for e in range(walk_slots)], axis=1)
        both = dot(left, jnp.concatenate(parts, axis=0))
        return both + pltpu.roll(both, HD, 1)

    def walk_pair(window, j):
        low = walk_rows(window, j)
        high = walk_rows(window, j + half)
        return jnp.where(lane < HD, low, high).astype(jnp.bfloat16)

    wait_recv(state_copies)

    def step_one(j, carry):
        pair = walk_pair(win0, j)
        win1[R * half + j] = pair
        f1[me_feat * half + j] = pair
        return carry

    lax.fori_loop(0, half, step_one, 0)
    one_copies = to_dom(win1, half, one_send, one_recv)
    start(one_copies)
    f1_copies = to_feat(f1, half, f1_send, f1_recv)
    start(f1_copies)
    kv_copies = to_dom(kv, 2 * blocks, kv_send, kv_recv)
    start(kv_copies)

    own = pl.ds(pl.multiple_of(me_feat * BS, BS), BS)
    bw[me_feat, 0] = bias_query[:, :, own]
    bw[me_feat, 1] = bias_key[:, :, own]
    wait_recv(bw_copies)
    zero = jnp.zeros((HD, BS), jnp.bfloat16)

    def spread(g, carry):
        for t in range(2):
            for s in range(2):
                weight = bw[g, t, s]
                wbd[g, t, pl.ds(s * BS, HD), :] = jnp.concatenate([weight, zero], axis=1)
                wbd[g, t, pl.ds(s * BS + HD, HD), :] = jnp.concatenate([zero, weight], axis=1)
        return carry

    lax.fori_loop(0, n_feat, spread, 0)

    wait_recv(one_copies)

    def step_two(j, carry):
        pair = walk_pair(win1, j)
        f2[me_feat * half + j] = pair
        walk_next[pl.ds(pl.multiple_of(j * BS, BS), BS), :] = pair[:, :HD]
        walk_next[pl.ds(pl.multiple_of((j + half) * BS, BS), BS), :] = pair[:, HD:]
        return carry

    lax.fori_loop(0, half, step_two, 0)
    f2_copies = to_feat(f2, half, f2_send, f2_recv)
    start(f2_copies)
    wait_recv(f1_copies)
    wait_recv(f2_copies)

    def bias(j, carry):
        sums = [None, None]
        for g in range(n_feat):
            feats = jnp.concatenate([f1[g * half + j], f2[g * half + j]], axis=1)
            for t in range(2):
                term = dot(feats, wbd[g, t]).astype(jnp.bfloat16).astype(jnp.float32)
                sums[t] = term if sums[t] is None else sums[t] + term
        bias_q, bias_k = sums[0].astype(jnp.bfloat16), sums[1].astype(jnp.bfloat16)
        biasq[j] = bias_q[:, :BS]
        biasq[j + half] = bias_q[:, BS:]
        bk[R * blocks + j] = bias_k[:, :BS]
        bk[R * blocks + j + half] = bias_k[:, BS:]
        return carry

    lax.fori_loop(0, half, bias, 0)
    bk_copies = to_dom(bk, blocks, bk_send, bk_recv)
    start(bk_copies)
    wait_recv(kv_copies)
    wait_recv(bk_copies)

    def out_copies(b):
        return [
            pltpu.make_async_remote_copy(
                src_ref=stage.at[b * n_feat + peer],
                dst_ref=landed.at[b * (n_feat - 1) + i],
                send_sem=out_send.at[b, i],
                recv_sem=out_recv.at[b, i],
                device_id={"feat": peer},
                device_id_type=MESH,
            )
            for i, peer in enumerate(peers)
        ]

    first_head = jnp.where(lane < HD, 1.0, 0.0).astype(jnp.bfloat16)
    second_head = jnp.where(lane < HD, 0.0, 1.0).astype(jnp.bfloat16)

    def attend(b, carry):
        count = attn_count[b]
        query, bias_q = queries[b], biasq[b]
        both = jnp.concatenate(
            [
                jnp.concatenate([query * first_head, bias_q * first_head], axis=1),
                jnp.concatenate([query * second_head, bias_q * second_head], axis=1),
            ],
            axis=0,
        )
        scores, near_values = [], []
        for e in range(attn_slots):
            pos = place(attn_cols[b, e])
            at = lax.div(pos, blocks) * (2 * blocks) + lax.rem(pos, blocks)
            key = jnp.concatenate([kv[at], bk[pos]], axis=1)
            near_values.append(kv[at + blocks])
            score = dot_t(both, key)
            scores.append(jnp.where(e < count, score, -1e30))
        scores = jnp.concatenate(scores, axis=1)
        top = jnp.max(scores, axis=1, keepdims=True)
        expo = jnp.exp2((scores - top) * (LOG2E * HD ** (-0.5)))
        weights = (expo * (1.0 / jnp.sum(expo, axis=1, keepdims=True))).astype(jnp.bfloat16)
        mixed = dot(weights, jnp.concatenate(near_values, axis=0))
        attended = jnp.where(lane < HD, mixed[:BS], mixed[BS:]).astype(jnp.bfloat16)
        term = dot(attended, w_out[...]).astype(jnp.bfloat16)
        for p in range(n_feat):
            stage[b * n_feat + p] = term[:, p * BS : (p + 1) * BS]
        start(out_copies(b))
        return carry

    lax.fori_loop(0, blocks, attend, 0)

    def finish(b, carry):
        copies = out_copies(b)
        wait_recv(copies)
        total_out = stage[b * n_feat + me_feat].astype(jnp.float32)
        for i in range(n_feat - 1):
            total_out += landed[b * (n_feat - 1) + i].astype(jnp.float32)
        new_nodes[pl.ds(pl.multiple_of(b * BS, BS), BS), :] = total_out.astype(jnp.bfloat16)
        for copy in copies:
            copy.wait_send()
        return carry

    lax.fori_loop(0, blocks, finish, 0)
    for copies in (state_copies, bw_copies, one_copies, f1_copies, kv_copies, f2_copies, bk_copies):
        for copy in copies:
            copy.wait_send()


def on_device(
    nodes,
    walk_state,
    walk_values,
    walk_cols,
    walk_count,
    attn_cols,
    attn_count,
    w_query,
    w_key,
    w_value,
    bias_query,
    bias_key,
    w_out,
):
    n_dom, n_feat = lax.axis_size("dom"), lax.axis_size("feat")
    blocks, walk_slots = walk_values.shape[:2]
    attn_slots = attn_cols.shape[1]
    rows, width = nodes.shape[0], w_out.shape[1] // n_feat
    half = blocks // 2
    wide = 2 * R + 1
    bf16 = jnp.bfloat16
    dma = pltpu.SemaphoreType.DMA
    smem = pl.BlockSpec(memory_space=pltpu.SMEM)
    vmem = pl.BlockSpec(memory_space=pltpu.VMEM)
    sizes = (n_dom, n_feat, blocks, walk_slots, attn_slots)
    return pl.pallas_call(
        functools.partial(kernel, sizes),
        out_shape=(
            jax.ShapeDtypeStruct((rows, width), bf16),
            jax.ShapeDtypeStruct(walk_state.shape, bf16),
        ),
        in_specs=[smem] * 4 + [vmem] * 9,
        out_specs=(vmem, vmem),
        scratch_shapes=[
            pltpu.VMEM((wide * half, BS, BS), bf16),
            pltpu.VMEM((wide * half, BS, BS), bf16),
            pltpu.VMEM((wide * 2 * blocks, BS, BS), bf16),
            pltpu.VMEM((wide * blocks, BS, BS), bf16),
            pltpu.VMEM((n_feat * half, BS, BS), bf16),
            pltpu.VMEM((n_feat * half, BS, BS), bf16),
            pltpu.VMEM((n_feat, 2, 2, HD, BS), bf16),
            pltpu.VMEM((n_feat, 2, 2 * BS, 2 * BS), bf16),
            pltpu.VMEM((blocks, BS, BS), bf16),
            pltpu.VMEM((blocks, BS, BS), bf16),
            pltpu.VMEM((blocks * n_feat, BS, BS), bf16),
            pltpu.VMEM((blocks * (n_feat - 1), BS, BS), bf16),
            dma((2 * R,)),
            dma((2 * R,)),
            dma((2 * R,)),
            dma((2 * R,)),
            dma((2 * R,)),
            dma((2 * R,)),
            dma((2 * R,)),
            dma((2 * R,)),
            dma((n_feat - 1,)),
            dma((n_feat - 1,)),
            dma((n_feat - 1,)),
            dma((n_feat - 1,)),
            dma((2, n_feat - 1)),
            dma((2, n_feat - 1)),
            dma((blocks, n_feat - 1)),
            dma((blocks, n_feat - 1)),
        ],
        compiler_params=pltpu.CompilerParams(
            collective_id=0, has_side_effects=True, vmem_limit_bytes=40 * 1024 * 1024
        ),
    )(
        walk_cols,
        walk_count,
        attn_cols,
        attn_count,
        nodes,
        walk_state,
        walk_values,
        w_query,
        w_key,
        w_value,
        bias_query,
        bias_key,
        w_out,
    )


def solution(mesh):
    placed = (
        P("dom", None),
        P("dom", "feat"),
        P("dom", None, None, None),
        P("dom", None),
        P("dom"),
        P("dom", None),
        P("dom"),
        P(None, "feat"),
        P(None, "feat"),
        P(None, "feat"),
        P(None, "feat", None),
        P(None, "feat", None),
        P("feat", None),
    )
    return jax.shard_map(
        on_device,
        mesh=mesh,
        in_specs=placed,
        out_specs=(P("dom", "feat"), P("dom", "feat")),
        check_vma=False,
    )
```

time: 246 us -> 107 us (0.43)
  the two profiles are of different devices: /device:TPU:0 before, /device:TPU:5 now
where the time goes in v1:
time: 107 us; the launch traced here: 106 us
  Pallas kernels  92 us (86%)
  local copies, waits for them, and re-layouts  13.5 us (13%)
    pallas_call x1, Pallas kernels, on_device(): pl.pallas_call(functools.partial(kernel, sizes), out_shape=(jax.ShapeDtyp...  92 us
    unnamed x26, local copies, waits for them, and re-layouts  12.7 us

profile of v1, /device:TPU:5, one launch (start us, length us, event | category | flops | bytes accessed | tf_op | source)
XLA Modules:
  0.0 106.1 jit_solution(15488333276427354172)
XLA Ops:
  0.6 1.1 %copy.15.walk_state = bf16[1024,64]{1,0:T(8,128)(2,1)S(1)} copy(bf16[1024,64]{0,1:T(8,128)(2,1)} %param.14) | data formatting | bytes 262144 | tf_op args[1]
  1.7 0.0 copy-start
  1.7 1.6 %copy-done = bf16[8,8,128,128]{3,2,1,0:T(8,128)(2,1)S(1)} copy-done((bf16[8,8,128,128]{3,2,1,0:T(8,128)(2,1)S(1)}, bf16[8,8,128,128]{3,2,1,0:T(8,128)(2,1)}, u32[]{:S(2)}) %copy-start) | copy-done | bytes 2097176
  3.3 0.0 copy-start.1
  3.3 1.2 %copy-done.1 = bf16[1024,512]{1,0:T(8,128)(2,1)S(1)} copy-done((bf16[1024,512]{1,0:T(8,128)(2,1)S(1)}, bf16[1024,512]{1,0:T(8,128)(2,1)}, u32[]{:S(2)}) %copy-start.1) | copy-done | bytes 1048600
  4.5 0.0 copy-start.2
  4.5 0.9 copy-done.2
  5.4 0.0 copy-start.3
  5.4 0.9 copy-done.3
  6.3 0.0 copy-start.4
  6.3 0.9 copy-done.4
  7.2 0.0 copy-start.5
  7.2 0.9 copy-done.5
  8.1 0.0 copy-start.6
  8.2 0.9 copy-done.6
  9.1 0.0 copy-start.7
  9.1 0.9 copy-done.7
  10.0 0.0 copy-start.8
  10.0 0.7 copy-done.8
  10.6 0.0 copy-start.9
  10.6 0.7 copy-done.9
  11.3 0.0 copy-start.10
  11.3 0.7 copy-done.10
  12.0 0.0 copy-start.11
  12.0 0.7 copy-done.11
  12.6 92.0 %shard_map.140 = (bf16[1024,128]{1,0:T(8,128)(2,1)S(1)}, bf16[1024,64]{1,0:T(8,128)(2,1)S(1)}) custom-call(s32[8,8]{1,0:T(8,128)S(1)} %copy-done.8, s32[8]{0:T(128)S(1)} %copy-done.10, s32[8,8]{1,0:T(8,128)S(1)} %copy-done.9, s32[8]{0:T(128)S(1)} %copy-done.11, bf16[1024,512]{1,0:T(8,128)(2,1)S(1)} %copy-done.1, bf16[1024,64]{1,0:T(8,128)(2,1)S(1)} %copy.15.walk_state, ...), custom_call_target="tpu_custom_call" | custom-call | tf_op jit(solution)/shard_map/pallas_call | solution.py:346
  104.6 0.8 copy.16
  105.4 0.7 copy.18
Async XLA Ops:
  1.7 1.6 %copy-start = (bf16[8,8,128,128]{3,2,1,0:T(8,128)(2,1)S(1)}, bf16[8,8,128,128]{3,2,1,0:T(8,128)(2,1)}, u32[]{:S(2)}) copy-start(bf16[8,8,128,128]{3,2,1,0:T(8,128)(2,1)} %walk_values.1) | copy-start | bytes 6291460
  3.3 1.2 %copy-start.1 = (bf16[1024,512]{1,0:T(8,128)(2,1)S(1)}, bf16[1024,512]{1,0:T(8,128)(2,1)}, u32[]{:S(2)}) copy-start(bf16[1024,512]{1,0:T(8,128)(2,1)} %nodes.1) | copy-start | bytes 3145732
  4.5 0.9 copy-start.2
  5.4 0.9 copy-start.3
  6.3 0.9 copy-start.4
  7.2 0.9 copy-start.5
  8.1 0.9 copy-start.6
  9.1 0.9 copy-start.7
  10.0 0.7 copy-start.8
  10.6 0.7 copy-start.9
  11.3 0.7 copy-start.10
  12.0 0.7 copy-start.11

commit v2 on v1

--- a/solution.py
+++ b/solution.py
@@ -11,7 +11,6 @@
 BS = 128
 R = 2
 MESH = pl.DeviceIdType.MESH
-OFFSETS = tuple(o for o in range(-R, R + 1) if o != 0)
 LOG2E = 1.4426950408889634
 
 
@@ -27,21 +26,31 @@
 
 def kernel(
     sizes,
+    walk_cols_hbm,
+    walk_count_hbm,
+    attn_cols_hbm,
+    attn_count_hbm,
+    nodes_hbm,
+    walk_state_hbm,
+    walk_values_hbm,
+    w_query_hbm,
+    w_key_hbm,
+    w_value_hbm,
+    bias_query_hbm,
+    bias_key_hbm,
+    w_out_hbm,
+    new_nodes,
+    walk_next,
     walk_cols,
     walk_count,
     attn_cols,
     attn_count,
-    nodes,
     walk_state,
     walk_values,
-    w_query,
-    w_key,
-    w_value,
-    bias_query,
-    bias_key,
+    w_all,
+    bias_maps,
     w_out,
-    new_nodes,
-    walk_next,
+    nwin,
     win0,
     win1,
     kv,
@@ -70,6 +79,15 @@
     bw_recv,
     out_send,
     out_recv,
+    node_send,
+    node_recv,
+    sib_send,
+    sib_recv,
+    far_send,
+    far_recv,
+    relay_send,
+    relay_recv,
+    local,
 ):
     n_dom, n_feat, blocks, walk_slots, attn_slots = sizes
     half = blocks // 2
@@ -78,7 +96,35 @@
     me_dom = lax.axis_index("dom")
     me_feat = lax.axis_index("feat")
     first = (me_dom - R) * blocks
-    near = [lax.rem(me_dom + o + n_dom, n_dom) for o in OFFSETS]
+    side = 1 - 2 * lax.rem(me_dom, 2)
+    offsets = (side, R, -R, -side)
+    arrivals = (R + side, 0, 2 * R, R - side)
+    near = [lax.rem(me_dom + o + n_dom, n_dom) for o in offsets]
+    sibling = me_feat + 1 - 2 * lax.rem(me_feat, 2)
+    across = lax.rem(me_feat + 2, n_feat)
+    diagonal = lax.rem(sibling + 2, n_feat)
+    loads = [
+        pltpu.make_async_copy(source, target, local.at[i])
+        for i, (source, target) in enumerate(
+            (
+                (walk_state_hbm, walk_state),
+                (bias_query_hbm, bias_maps.at[0]),
+                (bias_key_hbm, bias_maps.at[1]),
+                (nodes_hbm, nwin.at[pl.ds(R * n_feat, n_feat)]),
+                (w_query_hbm, w_all.at[:, pl.ds(0, BS)]),
+                (w_key_hbm, w_all.at[:, pl.ds(BS, BS)]),
+                (w_value_hbm, w_all.at[:, pl.ds(2 * BS, BS)]),
+                (walk_cols_hbm, walk_cols),
+                (walk_count_hbm, walk_count),
+                (walk_values_hbm, walk_values),
+                (w_out_hbm, w_out),
+                (attn_cols_hbm, attn_cols),
+                (attn_count_hbm, attn_count),
+            )
+        )
+    ]
+    for load in loads:
+        load.start()
     peers = [lax.rem(me_feat + d, n_feat) for d in range(1, n_feat)]
     lane = lax.broadcasted_iota(jnp.int32, (1, BS), 1)
     lane_half = lax.div(lane, HD)
@@ -89,7 +135,7 @@
 
     def to_dom(buffer, per, send, recv):
         copies = []
-        for i, o in enumerate(OFFSETS):
+        for i, o in enumerate(offsets):
             copies.append(
                 pltpu.make_async_remote_copy(
                     src_ref=buffer.at[pl.ds(R * per, per)],
@@ -126,9 +172,16 @@
         for copy in copies:
             copy.wait_recv()
 
-    win0[pl.ds(R * half, half)] = jnp.concatenate(
-        [walk_state[: half * BS, :], walk_state[half * BS :, :]], axis=1
-    ).reshape(half, BS, BS)
+    loads[0].wait()
+    for j in range(half):
+        columns = jnp.concatenate(
+            [
+                walk_state[:, j * BS : (j + 1) * BS],
+                walk_state[:, (j + half) * BS : (j + half + 1) * BS],
+            ],
+            axis=0,
+        )
+        win0[R * half + j] = columns.T
 
     barrier = pltpu.get_barrier_semaphore()
     for device in near:
@@ -139,12 +192,14 @@
 
     state_copies = to_dom(win0, half, state_send, state_recv)
     start(state_copies)
+    loads[1].wait()
+    loads[2].wait()
     bw_copies = []
-    for t, weight in enumerate((bias_query, bias_key)):
+    for t in range(2):
         for i, peer in enumerate(peers):
             bw_copies.append(
                 pltpu.make_async_remote_copy(
-                    src_ref=weight.at[:, :, pl.ds(pl.multiple_of(peer * BS, BS), BS)],
+                    src_ref=bias_maps.at[t, :, :, pl.ds(pl.multiple_of(peer * BS, BS), BS)],
                     dst_ref=bw.at[me_feat, t],
                     send_sem=bw_send.at[t, i],
                     recv_sem=bw_recv.at[t, i],
@@ -154,17 +209,24 @@
             )
     start(bw_copies)
 
-    w_all = jnp.concatenate([w_query[...], w_key[...], w_value[...]], axis=1)
+    for i in range(3, 7):
+        loads[i].wait()
+    per = blocks // n_feat
 
     def project(i, carry):
-        rows = nodes[pl.ds(pl.multiple_of(i * 2 * BS, 2 * BS), 2 * BS), :]
-        product = dot(rows, w_all).astype(jnp.bfloat16)
-        queries[pl.ds(2 * i, 2)] = product[:, :BS].reshape(2, BS, BS)
-        kv[pl.ds(2 * R * blocks + 2 * i, 2)] = product[:, BS : 2 * BS].reshape(2, BS, BS)
-        kv[pl.ds((2 * R + 1) * blocks + 2 * i, 2)] = product[:, 2 * BS :].reshape(2, BS, BS)
-        return carry
-
-    lax.fori_loop(0, blocks // 2, project, 0)
+        product = dot(nwin[R * n_feat + i], w_all[...]).astype(jnp.bfloat16)
+        queries[pl.ds(per * i, per)] = product[:, :BS].reshape(per, BS, BS)
+        kv[pl.ds(2 * R * blocks + per * i, per)] = product[:, BS : 2 * BS].reshape(per, BS, BS)
+        kv[pl.ds((2 * R + 1) * blocks + per * i, per)] = product[:, 2 * BS :].reshape(per, BS, BS)
+        return carry
+
+    lax.fori_loop(0, n_feat, project, 0)
+
+    def project_near(slot, quarter):
+        product = dot(nwin[slot * n_feat + quarter], w_all[:, BS:]).astype(jnp.bfloat16)
+        at = slot * 2 * blocks + per * quarter
+        kv[pl.ds(at, per)] = product[:, :BS].reshape(per, BS, BS)
+        kv[pl.ds(at + blocks, per)] = product[:, BS:].reshape(per, BS, BS)
 
     def walk_rows(window, b):
         count = walk_count[b]
@@ -173,8 +235,8 @@
             pos = place(walk_cols[b, e])
             part = lax.div(pos, blocks)
             block = lax.rem(pos, blocks)
-            side = jnp.where(e < count, lax.div(block, half), 2)
-            keep = jnp.where(lane_half == side, 1.0, 0.0).astype(jnp.bfloat16)
+            column_half = jnp.where(e < count, lax.div(block, half), 2)
+            keep = jnp.where(lane_half == column_half, 1.0, 0.0).astype(jnp.bfloat16)
             parts.append(window[part * half + lax.rem(block, half)] * keep)
         left = jnp.concatenate([walk_values[b, e] for e in range(walk_slots)], axis=1)
         both = dot(left, jnp.concatenate(parts, axis=0))
@@ -185,7 +247,27 @@
         high = walk_rows(window, j + half)
         return jnp.where(lane < HD, low, high).astype(jnp.bfloat16)
 
+    for i in range(7, 10):
+        loads[i].wait()
     wait_recv(state_copies)
+    node_copies = {}
+    for i in range(1, 4):
+        node_copies[i] = pltpu.make_async_remote_copy(
+            src_ref=nwin.at[R * n_feat + me_feat],
+            dst_ref=nwin.at[(R - offsets[i]) * n_feat + me_feat],
+            send_sem=node_send.at[i],
+            recv_sem=node_recv.at[i],
+            device_id={"dom": near[i]},
+            device_id_type=MESH,
+        )
+    kv_copy = pltpu.make_async_remote_copy(
+        src_ref=kv.at[pl.ds(R * 2 * blocks, 2 * blocks)],
+        dst_ref=kv.at[pl.ds((R - side) * 2 * blocks, 2 * blocks)],
+        send_sem=kv_send,
+        recv_sem=kv_recv,
+        device_id={"dom": near[0]},
+        device_id_type=MESH,
+    )
 
     def step_one(j, carry):
         pair = walk_pair(win0, j)
@@ -198,12 +280,12 @@
     start(one_copies)
     f1_copies = to_feat(f1, half, f1_send, f1_recv)
     start(f1_copies)
-    kv_copies = to_dom(kv, 2 * blocks, kv_send, kv_recv)
-    start(kv_copies)
+    start(node_copies.values())
+    kv_copy.start()
 
     own = pl.ds(pl.multiple_of(me_feat * BS, BS), BS)
-    bw[me_feat, 0] = bias_query[:, :, own]
-    bw[me_feat, 1] = bias_key[:, :, own]
+    bw[me_feat, 0] = bias_maps[0, :, :, own]
+    bw[me_feat, 1] = bias_maps[1, :, :, own]
     wait_recv(bw_copies)
     zero = jnp.zeros((HD, BS), jnp.bfloat16)
 
@@ -222,8 +304,9 @@
     def step_two(j, carry):
         pair = walk_pair(win1, j)
         f2[me_feat * half + j] = pair
-        walk_next[pl.ds(pl.multiple_of(j * BS, BS), BS), :] = pair[:, :HD]
-        walk_next[pl.ds(pl.multiple_of((j + half) * BS, BS), BS), :] = pair[:, HD:]
+        columns = pair.T
+        walk_next[:, pl.ds(pl.multiple_of(j * BS, BS), BS)] = columns[:HD]
+        walk_next[:, pl.ds(pl.multiple_of((j + half) * BS, BS), BS)] = columns[HD:]
         return carry
 
     lax.fori_loop(0, half, step_two, 0)
@@ -249,8 +332,42 @@
     lax.fori_loop(0, half, bias, 0)
     bk_copies = to_dom(bk, blocks, bk_send, bk_recv)
     start(bk_copies)
-    wait_recv(kv_copies)
+
+    def pass_on(i, quarter, target, send, recv):
+        return pltpu.make_async_remote_copy(
+            src_ref=nwin.at[arrivals[i] * n_feat + quarter],
+            dst_ref=nwin.at[arrivals[i] * n_feat + quarter],
+            send_sem=send.at[i],
+            recv_sem=recv.at[i],
+            device_id={"feat": target},
+            device_id_type=MESH,
+        )
+
+    shared = []
+    far, beside, relayed = {}, {}, {}
+    for i in range(1, 4):
+        node_copies[i].wait_recv()
+        far[i] = pass_on(i, me_feat, across, far_send, far_recv)
+        beside[i] = pass_on(i, me_feat, sibling, sib_send, sib_recv)
+        relayed[i] = pass_on(i, across, sibling, relay_send, relay_recv)
+        far[i].start()
+        beside[i].start()
+        project_near(arrivals[i], me_feat)
+    for i in range(1, 4):
+        far[i].wait_recv()
+        relayed[i].start()
+        project_near(arrivals[i], across)
+        beside[i].wait_recv()
+        project_near(arrivals[i], sibling)
+    for i in range(1, 4):
+        relayed[i].wait_recv()
+        project_near(arrivals[i], diagonal)
+    for copies in (far, beside, relayed):
+        shared += copies.values()
+    kv_copy.wait_recv()
     wait_recv(bk_copies)
+    for i in range(10, 13):
+        loads[i].wait()
 
     def out_copies(b):
         return [
@@ -312,9 +429,11 @@
         return carry
 
     lax.fori_loop(0, blocks, finish, 0)
-    for copies in (state_copies, bw_copies, one_copies, f1_copies, kv_copies, f2_copies, bk_copies):
+    for copies in (state_copies, bw_copies, one_copies, f1_copies, f2_copies, bk_copies):
         for copy in copies:
             copy.wait_send()
+    for copy in [kv_copy, *node_copies.values(), *shared]:
+        copy.wait_send()
 
 
 def on_device(
@@ -340,18 +459,28 @@
     wide = 2 * R + 1
     bf16 = jnp.bfloat16
     dma = pltpu.SemaphoreType.DMA
-    smem = pl.BlockSpec(memory_space=pltpu.SMEM)
+    hbm = pl.BlockSpec(memory_space=pltpu.HBM)
     vmem = pl.BlockSpec(memory_space=pltpu.VMEM)
     sizes = (n_dom, n_feat, blocks, walk_slots, attn_slots)
-    return pl.pallas_call(
+    out, next_columns = pl.pallas_call(
         functools.partial(kernel, sizes),
         out_shape=(
             jax.ShapeDtypeStruct((rows, width), bf16),
-            jax.ShapeDtypeStruct(walk_state.shape, bf16),
+            jax.ShapeDtypeStruct(walk_state.shape[::-1], bf16),
         ),
-        in_specs=[smem] * 4 + [vmem] * 9,
+        in_specs=[hbm] * 13,
         out_specs=(vmem, vmem),
         scratch_shapes=[
+            pltpu.SMEM(walk_cols.shape, jnp.int32),
+            pltpu.SMEM(walk_count.shape, jnp.int32),
+            pltpu.SMEM(attn_cols.shape, jnp.int32),
+            pltpu.SMEM(attn_count.shape, jnp.int32),
+            pltpu.VMEM(walk_state.shape[::-1], bf16),
+            pltpu.VMEM(walk_values.shape, bf16),
+            pltpu.VMEM((nodes.shape[1], 3 * BS), bf16),
+            pltpu.VMEM((2, *bias_query.shape), bf16),
+            pltpu.VMEM(w_out.shape, bf16),
+            pltpu.VMEM((wide * n_feat, rows // n_feat, nodes.shape[1]), bf16),
             pltpu.VMEM((wide * half, BS, BS), bf16),
             pltpu.VMEM((wide * half, BS, BS), bf16),
             pltpu.VMEM((wide * 2 * blocks, BS, BS), bf16),
@@ -368,8 +497,8 @@
             dma((2 * R,)),
             dma((2 * R,)),
             dma((2 * R,)),
-            dma((2 * R,)),
-            dma((2 * R,)),
+            dma(()),
+            dma(()),
             dma((2 * R,)),
             dma((2 * R,)),
             dma((n_feat - 1,)),
@@ -380,17 +509,26 @@
             dma((2, n_feat - 1)),
             dma((blocks, n_feat - 1)),
             dma((blocks, n_feat - 1)),
+            dma((2 * R,)),
+            dma((2 * R,)),
+            dma((2 * R,)),
+            dma((2 * R,)),
+            dma((2 * R,)),
+            dma((2 * R,)),
+            dma((2 * R,)),
+            dma((2 * R,)),
+            dma((13,)),
         ],
         compiler_params=pltpu.CompilerParams(
-            collective_id=0, has_side_effects=True, vmem_limit_bytes=40 * 1024 * 1024
+            collective_id=0, has_side_effects=True, vmem_limit_bytes=63 * 1024 * 1024
         ),
     )(
         walk_cols,
         walk_count,
         attn_cols,
         attn_count,
-        nodes,
-        walk_state,
+        nodes.reshape(n_feat, rows // n_feat, nodes.shape[1]),
+        walk_state.T,
         walk_values,
         w_query,
         w_key,
@@ -399,6 +537,7 @@
         bias_key,
         w_out,
     )
+    return out, next_columns.T
 
 
 def solution(mesh):

time: 107 us -> 83.8 us (0.78)
  the two profiles are of different devices: /device:TPU:5 before, /device:TPU:0 now
where the time goes in v2:
time: 83.8 us; the launch traced here: 83.6 us
  Pallas kernels  79.7 us (95%)
  local copies, waits for them, and re-layouts  3.24 us (4%)
    pallas_call x1, Pallas kernels, on_device(): pl.pallas_call(functools.partial(kernel, sizes), out_shape=(jax.ShapeDtyp...  79.7 us
    unnamed x2, local copies, waits for them, and re-layouts  3.24 us

profile of v2, /device:TPU:0, one launch (start us, length us, event | category | flops | bytes accessed | tf_op | source)
XLA Modules:
  0.0 83.6 jit_solution(12452402890981977819)
XLA Ops:
  0.6 79.7 %shard_map.140 = (bf16[1024,128]{1,0:T(8,128)(2,1)}, bf16[64,1024]{1,0:T(8,128)(2,1)}) custom-call(s32[8,8]{1,0:T(8,128)} %walk_cols_hbm.1, s32[8]{0:T(128)} %walk_count_hbm.1, s32[8,8]{1,0:T(8,128)} %attn_cols_hbm.1, s32[8]{0:T(128)} %attn_count_hbm.1, bf16[4,256,512]{2,1,0:T(8,128)(2,1)} %bitcast.3, bf16[64,1024]{1,0:T(8,128)(2,1)} %bitcast.4, ...), custom_call_target="tpu_custom_call" | custom-call | tf_op jit(solution)/shard_map/pallas_call | solution.py:465
  80.3 1.7 %copy.17 = bf16[1024,128]{1,0:T(8,128)(2,1)} copy(bf16[1024,128]{1,0:T(8,128)(2,1)} %get-tuple-element.8) | data formatting | bytes 524288
  82.0 1.6 %copy.18 = bf16[1024,64]{0,1:T(8,128)(2,1)} copy(bf16[1024,64]{0,1:T(8,128)(2,1)} %bitcast.5) | data formatting | bytes 262144

commit v3 on v2

--- a/solution.py
+++ b/solution.py
@@ -61,8 +61,8 @@
     wbd,
     queries,
     biasq,
-    stage,
-    landed,
+    att,
+    wo,
     state_send,
     state_recv,
     one_send,
@@ -88,6 +88,8 @@
     relay_send,
     relay_recv,
     local,
+    wo_send,
+    wo_recv,
 ):
     n_dom, n_feat, blocks, walk_slots, attn_slots = sizes
     half = blocks // 2
@@ -208,6 +210,19 @@
                 )
             )
     start(bw_copies)
+    loads[10].wait()
+    wo_copies = [
+        pltpu.make_async_remote_copy(
+            src_ref=w_out.at[:, pl.ds(pl.multiple_of(peer * BS, BS), BS)],
+            dst_ref=wo.at[me_feat],
+            send_sem=wo_send.at[i],
+            recv_sem=wo_recv.at[i],
+            device_id={"feat": peer},
+            device_id_type=MESH,
+        )
+        for i, peer in enumerate(peers)
+    ]
+    start(wo_copies)
 
     for i in range(3, 7):
         loads[i].wait()
@@ -286,6 +301,8 @@
     own = pl.ds(pl.multiple_of(me_feat * BS, BS), BS)
     bw[me_feat, 0] = bias_maps[0, :, :, own]
     bw[me_feat, 1] = bias_maps[1, :, :, own]
+    wo[me_feat] = w_out[:, own]
+    wait_recv(wo_copies)
     wait_recv(bw_copies)
     zero = jnp.zeros((HD, BS), jnp.bfloat16)
 
@@ -301,21 +318,47 @@
 
     wait_recv(one_copies)
 
+    def f2_copies(j):
+        at = me_feat * half + j
+        return [
+            pltpu.make_async_remote_copy(
+                src_ref=f2.at[at],
+                dst_ref=f2.at[at],
+                send_sem=f2_send.at[j, i],
+                recv_sem=f2_recv.at[j, i],
+                device_id={"feat": peer},
+                device_id_type=MESH,
+            )
+            for i, peer in enumerate(peers)
+        ]
+
+    def bk_copies(j):
+        return [
+            pltpu.make_async_remote_copy(
+                src_ref=bk.at[pl.ds(R * blocks + 2 * j, 2)],
+                dst_ref=bk.at[pl.ds((R - o) * blocks + 2 * j, 2)],
+                send_sem=bk_send.at[j, i],
+                recv_sem=bk_recv.at[j, i],
+                device_id={"dom": near[i]},
+                device_id_type=MESH,
+            )
+            for i, o in enumerate(offsets)
+        ]
+
     def step_two(j, carry):
         pair = walk_pair(win1, j)
         f2[me_feat * half + j] = pair
+        start(f2_copies(j))
         columns = pair.T
         walk_next[:, pl.ds(pl.multiple_of(j * BS, BS), BS)] = columns[:HD]
         walk_next[:, pl.ds(pl.multiple_of((j + half) * BS, BS), BS)] = columns[HD:]
         return carry
 
     lax.fori_loop(0, half, step_two, 0)
-    f2_copies = to_feat(f2, half, f2_send, f2_recv)
-    start(f2_copies)
     wait_recv(f1_copies)
-    wait_recv(f2_copies)
 
     def bias(j, carry):
+        wait_recv(f2_copies(j))
         sums = [None, None]
         for g in range(n_feat):
             feats = jnp.concatenate([f1[g * half + j], f2[g * half + j]], axis=1)
@@ -325,13 +368,12 @@
         bias_q, bias_k = sums[0].astype(jnp.bfloat16), sums[1].astype(jnp.bfloat16)
         biasq[j] = bias_q[:, :BS]
         biasq[j + half] = bias_q[:, BS:]
-        bk[R * blocks + j] = bias_k[:, :BS]
-        bk[R * blocks + j + half] = bias_k[:, BS:]
+        bk[R * blocks + 2 * j] = bias_k[:, :BS]
+        bk[R * blocks + 2 * j + 1] = bias_k[:, BS:]
+        start(bk_copies(j))
         return carry
 
     lax.fori_loop(0, half, bias, 0)
-    bk_copies = to_dom(bk, blocks, bk_send, bk_recv)
-    start(bk_copies)
 
     def pass_on(i, quarter, target, send, recv):
         return pltpu.make_async_remote_copy(
@@ -365,22 +407,33 @@
     for copies in (far, beside, relayed):
         shared += copies.values()
     kv_copy.wait_recv()
-    wait_recv(bk_copies)
-    for i in range(10, 13):
-        loads[i].wait()
-
-    def out_copies(b):
+
+    def bk_landed(j, carry):
+        wait_recv(bk_copies(j))
+        return carry
+
+    lax.fori_loop(0, half, bk_landed, 0)
+    loads[11].wait()
+    loads[12].wait()
+
+    def att_copies(b):
+        moves = ((me_feat, sibling), (me_feat, across), (across, sibling))
         return [
             pltpu.make_async_remote_copy(
-                src_ref=stage.at[b * n_feat + peer],
-                dst_ref=landed.at[b * (n_feat - 1) + i],
+                src_ref=att.at[group * blocks + b],
+                dst_ref=att.at[group * blocks + b],
                 send_sem=out_send.at[b, i],
                 recv_sem=out_recv.at[b, i],
-                device_id={"feat": peer},
+                device_id={"feat": target},
                 device_id_type=MESH,
             )
-            for i, peer in enumerate(peers)
+            for i, (group, target) in enumerate(moves)
         ]
+
+    def relay(b):
+        copies = att_copies(b)
+        copies[1].wait_recv()
+        copies[2].start()
 
     first_head = jnp.where(lane < HD, 1.0, 0.0).astype(jnp.bfloat16)
     second_head = jnp.where(lane < HD, 0.0, 1.0).astype(jnp.bfloat16)
@@ -398,8 +451,10 @@
         scores, near_values = [], []
         for e in range(attn_slots):
             pos = place(attn_cols[b, e])
-            at = lax.div(pos, blocks) * (2 * blocks) + lax.rem(pos, blocks)
-            key = jnp.concatenate([kv[at], bk[pos]], axis=1)
+            part, block = lax.div(pos, blocks), lax.rem(pos, blocks)
+            at = part * (2 * blocks) + block
+            bias_at = part * blocks + 2 * lax.rem(block, half) + lax.div(block, half)
+            key = jnp.concatenate([kv[at], bk[bias_at]], axis=1)
             near_values.append(kv[at + blocks])
             score = dot_t(both, key)
             scores.append(jnp.where(e < count, score, -1e30))
@@ -409,27 +464,48 @@
         weights = (expo * (1.0 / jnp.sum(expo, axis=1, keepdims=True))).astype(jnp.bfloat16)
         mixed = dot(weights, jnp.concatenate(near_values, axis=0))
         attended = jnp.where(lane < HD, mixed[:BS], mixed[BS:]).astype(jnp.bfloat16)
-        term = dot(attended, w_out[...]).astype(jnp.bfloat16)
-        for p in range(n_feat):
-            stage[b * n_feat + p] = term[:, p * BS : (p + 1) * BS]
-        start(out_copies(b))
-        return carry
-
+        att[me_feat * blocks + b] = attended
+        copies = att_copies(b)
+        copies[1].start()
+        copies[0].start()
+
+        @pl.when(b >= lag)
+        def _():
+            relay(b - lag)
+
+        return carry
+
+    lag = 2
     lax.fori_loop(0, blocks, attend, 0)
 
+    def relay_rest(b, carry):
+        relay(b)
+        return carry
+
+    lax.fori_loop(blocks - lag, blocks, relay_rest, 0)
+
     def finish(b, carry):
-        copies = out_copies(b)
-        wait_recv(copies)
-        total_out = stage[b * n_feat + me_feat].astype(jnp.float32)
-        for i in range(n_feat - 1):
-            total_out += landed[b * (n_feat - 1) + i].astype(jnp.float32)
+        copies = att_copies(b)
+        copies[0].wait_recv()
+        copies[2].wait_recv()
+        total_out = None
+        for g in range(n_feat):
+            term = dot(att[g * blocks + b], wo[g]).astype(jnp.bfloat16).astype(jnp.float32)
+            total_out = term if total_out is None else total_out + term
         new_nodes[pl.ds(pl.multiple_of(b * BS, BS), BS), :] = total_out.astype(jnp.bfloat16)
         for copy in copies:
             copy.wait_send()
         return carry
 
     lax.fori_loop(0, blocks, finish, 0)
-    for copies in (state_copies, bw_copies, one_copies, f1_copies, f2_copies, bk_copies):
+
+    def drain(j, carry):
+        for copy in f2_copies(j) + bk_copies(j):
+            copy.wait_send()
+        return carry
+
+    lax.fori_loop(0, half, drain, 0)
+    for copies in (state_copies, bw_copies, wo_copies, one_copies, f1_copies):
         for copy in copies:
             copy.wait_send()
     for copy in [kv_copy, *node_copies.values(), *shared]:
@@ -492,19 +568,19 @@
             pltpu.VMEM((blocks, BS, BS), bf16),
             pltpu.VMEM((blocks, BS, BS), bf16),
             pltpu.VMEM((blocks * n_feat, BS, BS), bf16),
-            pltpu.VMEM((blocks * (n_feat - 1), BS, BS), bf16),
+            pltpu.VMEM((n_feat, BS, BS), bf16),
             dma((2 * R,)),
             dma((2 * R,)),
             dma((2 * R,)),
             dma((2 * R,)),
             dma(()),
             dma(()),
-            dma((2 * R,)),
-            dma((2 * R,)),
+            dma((half, 2 * R)),
+            dma((half, 2 * R)),
             dma((n_feat - 1,)),
             dma((n_feat - 1,)),
-            dma((n_feat - 1,)),
-            dma((n_feat - 1,)),
+            dma((half, n_feat - 1)),
+            dma((half, n_feat - 1)),
             dma((2, n_feat - 1)),
             dma((2, n_feat - 1)),
             dma((blocks, n_feat - 1)),
@@ -518,6 +594,8 @@
             dma((2 * R,)),
             dma((2 * R,)),
             dma((13,)),
+            dma((n_feat - 1,)),
+            dma((n_feat - 1,)),
         ],
         compiler_params=pltpu.CompilerParams(
             collective_id=0, has_side_effects=True, vmem_limit_bytes=63 * 1024 * 1024

time: 83.8 us -> 85.8 us (1.024)
  Pallas kernels: 79.7 us -> 81.7 us
    pallas_call x1, Pallas kernels: 79.7 us -> 81.7 us  [on_device(): pl.pallas_call(functools.partial(kernel, sizes), out_shape=(jax.ShapeDtyp...]
where the time goes in v3:
time: 85.8 us; the launch traced here: 85.6 us
  Pallas kernels  81.7 us (95%)
  local copies, waits for them, and re-layouts  3.24 us (4%)
    pallas_call x1, Pallas kernels, on_device(): pl.pallas_call(functools.partial(kernel, sizes), out_shape=(jax.ShapeDtyp...  81.7 us
    unnamed x2, local copies, waits for them, and re-layouts  3.24 us

profile of v3, /device:TPU:0, one launch (start us, length us, event | category | flops | bytes accessed | tf_op | source)
XLA Modules:
  0.0 85.6 jit_solution(7755668680412603342)
XLA Ops:
  0.6 81.7 %shard_map.140 = (bf16[1024,128]{1,0:T(8,128)(2,1)}, bf16[64,1024]{1,0:T(8,128)(2,1)}) custom-call(s32[8,8]{1,0:T(8,128)} %walk_cols_hbm.1, s32[8]{0:T(128)} %walk_count_hbm.1, s32[8,8]{1,0:T(8,128)} %attn_cols_hbm.1, s32[8]{0:T(128)} %attn_count_hbm.1, bf16[4,256,512]{2,1,0:T(8,128)(2,1)} %bitcast.3, bf16[64,1024]{1,0:T(8,128)(2,1)} %bitcast.4, ...), custom_call_target="tpu_custom_call" | custom-call | tf_op jit(solution)/shard_map/pallas_call | solution.py:541
  82.4 1.7 %copy.17 = bf16[1024,128]{1,0:T(8,128)(2,1)} copy(bf16[1024,128]{1,0:T(8,128)(2,1)} %get-tuple-element.8) | data formatting | bytes 524288
  84.0 1.6 %copy.18 = bf16[1024,64]{0,1:T(8,128)(2,1)} copy(bf16[1024,64]{0,1:T(8,128)(2,1)} %bitcast.5) | data formatting | bytes 262144

commit v4 on v2

--- a/solution.py
+++ b/solution.py
@@ -269,6 +269,9 @@
         device_id_type=MESH,
     )
 
+    start(node_copies.values())
+    kv_copy.start()
+
     def step_one(j, carry):
         pair = walk_pair(win0, j)
         win1[R * half + j] = pair
@@ -280,8 +283,6 @@
     start(one_copies)
     f1_copies = to_feat(f1, half, f1_send, f1_recv)
     start(f1_copies)
-    start(node_copies.values())
-    kv_copy.start()
 
     own = pl.ds(pl.multiple_of(me_feat * BS, BS), BS)
     bw[me_feat, 0] = bias_maps[0, :, :, own]

time: 83.8 us -> 94.7 us (1.13)
  Pallas kernels: 79.7 us -> 90.7 us
    pallas_call x1, Pallas kernels: 79.7 us -> 90.7 us  [on_device(): pl.pallas_call(functools.partial(kernel, sizes), out_shape=(jax.ShapeDtyp...]
where the time goes in v4:
time: 94.7 us; the launch traced here: 94.5 us
  Pallas kernels  90.7 us (96%)
  local copies, waits for them, and re-layouts  3.24 us (3%)
    pallas_call x1, Pallas kernels, on_device(): pl.pallas_call(functools.partial(kernel, sizes), out_shape=(jax.ShapeDtyp...  90.7 us
    unnamed x2, local copies, waits for them, and re-layouts  3.24 us

profile of v4, /device:TPU:0, one launch (start us, length us, event | category | flops | bytes accessed | tf_op | source)
XLA Modules:
  0.0 94.5 jit_solution(3521346212175623034)
XLA Ops:
  0.6 90.7 %shard_map.140 = (bf16[1024,128]{1,0:T(8,128)(2,1)}, bf16[64,1024]{1,0:T(8,128)(2,1)}) custom-call(s32[8,8]{1,0:T(8,128)} %walk_cols_hbm.1, s32[8]{0:T(128)} %walk_count_hbm.1, s32[8,8]{1,0:T(8,128)} %attn_cols_hbm.1, s32[8]{0:T(128)} %attn_count_hbm.1, bf16[4,256,512]{2,1,0:T(8,128)(2,1)} %bitcast.3, bf16[64,1024]{1,0:T(8,128)(2,1)} %bitcast.4, ...), custom_call_target="tpu_custom_call" | custom-call | tf_op jit(solution)/shard_map/pallas_call | solution.py:466
  91.3 1.7 %copy.17 = bf16[1024,128]{1,0:T(8,128)(2,1)} copy(bf16[1024,128]{1,0:T(8,128)(2,1)} %get-tuple-element.8) | data formatting | bytes 524288
  93.0 1.6 %copy.18 = bf16[1024,64]{0,1:T(8,128)(2,1)} copy(bf16[1024,64]{0,1:T(8,128)(2,1)} %bitcast.5) | data formatting | bytes 262144
